TPU v7x, 32 devices: a whole 2x2x4 slice. The times are simulated.
32 devices in a mesh: dp: 8 (over y, x, core), mp: 4 (over z).
Axes of the slice: x: 2, y: 2, z: 4, core: 2. Of those that a mesh axis runs over, the one named last changes fastest.
Arguments:
- pyramid: bfloat16 [32, 5440, 256], P(('dp', 'mp')), may hold values from -6 to 6
- proposals: int32 [32, 4, 128], P(('dp', 'mp')), may hold values from 0 to 256, as said below
- levels: int32 [32, 128], P(('dp', 'mp')), may hold values from 0 to 3
- labels: int32 [32, 128], P(('dp', 'mp')), may hold values from 0 to 80, as said below
- targets: int32 [32, 4, 128], P(('dp', 'mp')), may hold values from -64 to 320, as said below
- buckets: int32 [32], P(('dp', 'mp')), may hold values from 0 to 4, as said below
- first_weight: bfloat16 [2, 12544, 1024], P(None, None, 'mp'), may hold values from -0.0546875 to 0.0546875
- first_bias: float32 [2, 1024], replicated, may hold values from -3 to 3
- second_weight: bfloat16 [2, 1024, 1024], replicated, may hold values from -0.1875 to 0.1875
- second_bias: float32 [2, 1024], replicated, may hold values from -3 to 3
- class_weight: bfloat16 [2, 1024, 81], replicated, may hold values from -0.5 to 0.5
- class_bias: float32 [2, 81], replicated, may hold values from -3 to 3
- box_weight: bfloat16 [2, 1024, 4], replicated, may hold values from -0.75 to 0.75
- box_bias: float32 [2, 4], replicated, may hold values from -2 to 2
Outputs:
- scores: float32 [32, 128, 81], P(('dp', 'mp'))
- decoded: float32 [32, 4, 128], P(('dp', 'mp'))
- pyramid_grad: float32 [32, 5440, 256], P(('dp', 'mp'))
- first_weight_grad: float32 [2, 12544, 1024], P(None, None, 'mp')
- first_bias_grad: float32 [2, 1024], replicated
- second_weight_grad: float32 [2, 1024, 1024], replicated
- second_bias_grad: float32 [2, 1024], replicated
- class_weight_grad: float32 [2, 1024, 81], replicated
- class_bias_grad: float32 [2, 81], replicated
- box_weight_grad: float32 [2, 1024, 4], replicated
- box_bias_grad: float32 [2, 4], replicated
Inputs may be any that keep to these rules, and one draw needn't show every extreme that they name: `buckets`: some image has bucket 0 and another bucket 4. `proposals`: each box lies in its image, 256 pixels wide and 128 + b * (32) high for bucket b, and is 8 pixels or more wide and high. `targets`: each target is its proposal with every edge moved by at most a quarter of the proposal's extent along that axis. `labels`: 0 is background.
All inputs are finite; a program needn't handle non-finite values.
Results may differ from a plain program's by a relative error of at most 0.033.
Values may be sent and summed in bfloat16 or wider, within the bound.
A program may use at most 384 MiB of HBM per device.

v0:
```python
import math

import jax
import jax.numpy as jnp
from jax import lax
from jax.sharding import PartitionSpec as P

CH = 256
CLS = 81
POOL = 7
CANVAS = 256
FEAT = 12544


def level_sides():
    return [CANVAS // (4 << level_no) for level_no in range(4)]


def level_tables(corners, level_ids):
    stride_list = [4 << level_no for level_no in range(4)]
    side_list = level_sides()
    onehot = level_ids[:, None] == jnp.arange(4, dtype=jnp.int32)[None, :]
    inverse = jnp.sum(
        jnp.where(
            onehot,
            jnp.array([1.0 / stride_value for stride_value in stride_list], jnp.float32)[None, :],
            0.0,
        ),
        axis=1,
    )
    side_cells = jnp.sum(jnp.where(onehot, jnp.array(side_list, jnp.int32)[None, :], 0), axis=1)
    fractions = (jnp.arange(POOL, dtype=jnp.float32) + 0.5) / POOL

    def axis_points(begin, finish):
        points = (begin[:, None] + fractions[None, :] * (finish - begin)[:, None]) * inverse[
            :, None
        ] - 0.5
        points = jnp.clip(points, 0.0, (side_cells - 1).astype(points.dtype)[:, None])
        lower_cell = jnp.minimum(jnp.floor(points).astype(jnp.int32), side_cells[:, None] - 2)
        return (lower_cell, points - lower_cell.astype(points.dtype))

    col_low, col_frac = axis_points(corners[0], corners[2])
    row_low, row_frac = axis_points(corners[1], corners[3])
    row_tables = []
    col_tables = []
    for level_no in range(4):
        span = jnp.arange(side_list[level_no], dtype=jnp.int32)[None, None, :]
        member = onehot[:, level_no].astype(jnp.float32)[:, None, None]

        def spread_table(lower_cell, frac):
            upper = jnp.where(span == lower_cell[:, :, None], 1.0 - frac[:, :, None], 0.0)
            upper = upper + jnp.where(span == lower_cell[:, :, None] + 1, frac[:, :, None], 0.0)
            return member * upper

        row_tables.append(spread_table(row_low, row_frac))
        col_tables.append(spread_table(col_low, col_frac))
    return (tuple(row_tables), tuple(col_tables))


def level_maps(feature):
    side_list = level_sides()
    maps_all = []
    offset = 0
    for side_value in side_list:
        maps_all.append(
            feature[offset : offset + side_value * side_value]
            .astype(jnp.float32)
            .reshape(side_value, side_value, CH)
        )
        offset = offset + side_value * side_value
    return maps_all


def block_split(tables, block):
    return tuple(
        (table.reshape(table.shape[0] // block, block, POOL, table.shape[2]) for table in tables)
    )


def pool_rows(maps_all, row_tables, col_tables):
    regions = row_tables[0].shape[0]
    block = math.gcd(regions, 64)

    def pool_one_block(parts):
        rows_part, cols_part = parts
        total = jnp.zeros((block, POOL, POOL, CH), jnp.float32)
        for level_no in range(4):
            middle = jnp.einsum(
                "ris,stk->ritk",
                rows_part[level_no],
                maps_all[level_no],
                precision=lax.Precision.HIGHEST,
            )
            total = total + jnp.einsum(
                "ritk,rjt->rijk", middle, cols_part[level_no], precision=lax.Precision.HIGHEST
            )
        return total

    pooled = lax.map(
        pool_one_block, (block_split(row_tables, block), block_split(col_tables, block))
    )
    return pooled.reshape(regions, POOL * POOL * CH)


def spread_back(gradient, row_tables, col_tables):
    regions = row_tables[0].shape[0]
    block = math.gcd(regions, 64)
    side_list = level_sides()
    grads_part = gradient.reshape(regions // block, block, POOL, POOL, CH)
    start = tuple(
        (jnp.zeros((side_value, side_value, CH), jnp.float32) for side_value in side_list)
    )

    def spread_one_block(running, parts):
        rows_part, cols_part, grad_part = parts
        updated = []
        for level_no in range(4):
            middle = jnp.einsum(
                "rijk,rjt->ritk", grad_part, cols_part[level_no], precision=lax.Precision.HIGHEST
            )
            updated.append(
                running[level_no]
                + jnp.einsum(
                    "ris,ritk->stk", rows_part[level_no], middle, precision=lax.Precision.HIGHEST
                )
            )
        return (tuple(updated), None)

    totals, unused_rest = lax.scan(
        spread_one_block,
        start,
        (block_split(row_tables, block), block_split(col_tables, block), grads_part),
    )
    return jnp.concatenate([totals[level_no].reshape(-1, CH) for level_no in range(4)], axis=0)


def box_frame(corners):
    box_width = corners[2] - corners[0]
    box_height = corners[3] - corners[1]
    return (corners[0] + 0.5 * box_width, corners[1] + 0.5 * box_height, box_width, box_height)


def encode_boxes(corners, truth_boxes, factor):
    centre_col, centre_row, box_width, box_height = box_frame(corners)
    truth_col, truth_row, truth_width, truth_height = box_frame(truth_boxes)
    return jnp.stack(
        [
            10.0 * factor * (truth_col - centre_col) / box_width,
            10.0 * factor * (truth_row - centre_row) / box_height,
            5.0 * factor * jnp.log(truth_width / box_width),
            5.0 * factor * jnp.log(truth_height / box_height),
        ],
        axis=1,
    )


def decode_boxes(corners, deltas, factor):
    centre_col, centre_row, box_width, box_height = box_frame(corners)
    moved_col = centre_col + deltas[:, 0] / (10.0 * factor) * box_width
    moved_row = centre_row + deltas[:, 1] / (10.0 * factor) * box_height
    moved_width = box_width * jnp.exp(deltas[:, 2] / (5.0 * factor))
    moved_height = box_height * jnp.exp(deltas[:, 3] / (5.0 * factor))
    return jnp.stack(
        [
            moved_col - 0.5 * moved_width,
            moved_row - 0.5 * moved_height,
            moved_col + 0.5 * moved_width,
            moved_row + 0.5 * moved_height,
        ],
        axis=0,
    )


def gelu_grad(preact, upstream):
    unused_value, pullback = jax.vjp(jax.nn.gelu, preact)
    return pullback(upstream.astype(jnp.float32))[0]


def per_device(
    pyramid,
    proposals,
    levels,
    labels,
    targets,
    buckets,
    first_weight,
    first_bias,
    second_weight,
    second_bias,
    class_weight,
    class_bias,
    box_weight,
    box_bias,
):
    maps_all = level_maps(pyramid[0])
    level_ids = levels[0]
    label_ids = labels[0]
    truth_boxes = targets[0].astype(jnp.float32)
    regions = level_ids.shape[0]
    slice_width = first_weight.shape[2]
    live_rows = jnp.arange(regions, dtype=jnp.int32) < regions // 2 + buckets[0] * (regions // 8)
    live_count = jnp.sum(live_rows.astype(jnp.float32))
    onehot = (label_ids[:, None] == jnp.arange(CLS, dtype=jnp.int32)[None, :]).astype(jnp.float32)
    moving = jnp.logical_and(live_rows, label_ids > 0).astype(jnp.float32)

    def fold_columns(running, shard_piece, dfirst_pre):
        for block_no in range(shard_piece.shape[1] // slice_width):
            cols_part = lax.dynamic_slice_in_dim(dfirst_pre, block_no * slice_width, slice_width, 1)
            part_sum = jnp.einsum(
                "rh,fh->rf",
                cols_part,
                shard_piece[:, block_no * slice_width : (block_no + 1) * slice_width],
                preferred_element_type=jnp.float32,
            )
            running = running + lax.optimization_barrier(part_sum.astype(jnp.bfloat16)).astype(
                jnp.float32
            )
        return running

    def forward_section(section_no, corners):
        row_tables, col_tables = level_tables(corners, level_ids)
        pooled = pool_rows(maps_all, row_tables, col_tables).astype(jnp.bfloat16)
        first_pre = (
            jnp.dot(
                pooled,
                lax.all_gather(first_weight[section_no], "mp", axis=1, tiled=True),
                preferred_element_type=jnp.float32,
            )
            + first_bias[section_no]
        )
        first_act = jax.nn.gelu(first_pre).astype(jnp.bfloat16)
        second_pre = (
            jnp.dot(first_act, second_weight[section_no], preferred_element_type=jnp.float32)
            + second_bias[section_no]
        )
        second_act = jax.nn.gelu(second_pre).astype(jnp.bfloat16)
        logits = (
            jnp.dot(second_act, class_weight[section_no], preferred_element_type=jnp.float32)
            + class_bias[section_no]
        )
        deltas = (
            jnp.dot(second_act, box_weight[section_no], preferred_element_type=jnp.float32)
            + box_bias[section_no]
        )
        return (
            row_tables,
            col_tables,
            pooled,
            first_pre,
            first_act,
            second_pre,
            second_act,
            logits,
            deltas,
        )

    def backward_section(section_no, saved_values, corners):
        (
            row_tables,
            col_tables,
            pooled,
            first_pre,
            first_act,
            second_pre,
            second_act,
            logits,
            deltas,
        ) = saved_values
        goal_deltas = encode_boxes(corners, truth_boxes, section_no + 1.0)
        class_probs = jax.nn.softmax(logits, axis=1)
        dlogits = (
            live_rows.astype(jnp.float32)[:, None] * (class_probs - onehot) / live_count
        ).astype(jnp.bfloat16)
        ddeltas = (moving[:, None] * jnp.clip(deltas - goal_deltas, -1.0, 1.0) / live_count).astype(
            jnp.bfloat16
        )
        class_grad = jnp.einsum(
            "rh,rc->hc", second_act, dlogits, preferred_element_type=jnp.float32
        )
        class_bias_grad = jnp.sum(dlogits.astype(jnp.float32), axis=0)
        box_grad = jnp.einsum("rh,rc->hc", second_act, ddeltas, preferred_element_type=jnp.float32)
        box_bias_grad = jnp.sum(ddeltas.astype(jnp.float32), axis=0)
        dsecond_act = jnp.einsum(
            "rc,hc->rh", dlogits, class_weight[section_no], preferred_element_type=jnp.float32
        ) + jnp.einsum(
            "rc,hc->rh", ddeltas, box_weight[section_no], preferred_element_type=jnp.float32
        )
        dsecond_pre = gelu_grad(second_pre, dsecond_act).astype(jnp.bfloat16)
        second_grad = jnp.einsum(
            "rh,rk->hk", first_act, dsecond_pre, preferred_element_type=jnp.float32
        )
        second_bias_grad = jnp.sum(dsecond_pre.astype(jnp.float32), axis=0)
        dfirst_act = jnp.einsum(
            "rk,hk->rh", dsecond_pre, second_weight[section_no], preferred_element_type=jnp.float32
        ).astype(jnp.bfloat16)
        dfirst_pre = gelu_grad(first_pre, dfirst_act).astype(jnp.bfloat16)
        first_bias_grad = jnp.sum(dfirst_pre.astype(jnp.float32), axis=0)
        whole_grad = jnp.einsum("rf,rh->fh", pooled, dfirst_pre, preferred_element_type=jnp.float32)
        first_grad = lax.psum_scatter(
            whole_grad.astype(jnp.bfloat16), "mp", scatter_dimension=1, tiled=True
        ).astype(jnp.float32)
        empty = jnp.zeros((regions, FEAT), jnp.float32)
        dpooled = fold_columns(
            empty, lax.all_gather(first_weight[section_no], "mp", axis=1, tiled=True), dfirst_pre
        )
        pyramid_part = spread_back(dpooled, row_tables, col_tables)
        grads_all = (
            first_grad,
            first_bias_grad,
            second_grad,
            second_bias_grad,
            class_grad,
            class_bias_grad,
            box_grad,
            box_bias_grad,
        )
        return (class_probs, grads_all, pyramid_part)

    first_corners = proposals[0].astype(jnp.float32)
    first_saved = forward_section(0, first_corners)
    second_corners = decode_boxes(first_corners, first_saved[8], 1.0)
    second_saved = forward_section(1, second_corners)
    decoded = decode_boxes(second_corners, second_saved[8], 2.0)
    class_probs, second_grads, second_pyramid = backward_section(1, second_saved, second_corners)
    unused_probs, first_grads, first_pyramid = backward_section(0, first_saved, first_corners)
    stacked = [jnp.stack([first_grads[member], second_grads[member]]) for member in range(8)]
    weight_total = lax.psum(stacked[0].astype(jnp.bfloat16), "dp").astype(jnp.float32)
    head_totals = lax.psum(
        (stacked[1], stacked[2], stacked[3], stacked[4], stacked[5], stacked[6], stacked[7]),
        ("dp", "mp"),
    )
    pyramid_grad = ((first_pyramid + second_pyramid) / 3.0)[None]
    return (
        class_probs[None],
        decoded[None],
        pyramid_grad,
        weight_total,
        head_totals[0],
        head_totals[1],
        head_totals[2],
        head_totals[3],
        head_totals[4],
        head_totals[5],
        head_totals[6],
    )


def solution(mesh):
    return jax.shard_map(
        per_device,
        mesh=mesh,
        in_specs=(
            P(("dp", "mp"), None, None),
            P(("dp", "mp"), None, None),
            P(("dp", "mp"), None),
            P(("dp", "mp"), None),
            P(("dp", "mp"), None, None),
            P(("dp", "mp")),
            P(None, None, "mp"),
            P(),
            P(),
            P(),
            P(),
            P(),
            P(),
            P(),
        ),
        out_specs=(
            P(("dp", "mp"), None, None),
            P(("dp", "mp"), None, None),
            P(("dp", "mp"), None, None),
            P(None, None, "mp"),
            P(),
            P(),
            P(),
            P(),
            P(),
            P(),
            P(),
        ),
        check_vma=False,
    )
```

profile of v0, /device:TPU:0, one launch (start us, length us, event | category | flops | bytes accessed | tf_op | source)
XLA Modules:
  0.0 2174.0 jit_solution(5699725835851410851)
XLA Ops:
  36.3 265.6 %while.54 = (s32[]{:T(128)}, bf16[2,64,7,7,256]{4,3,2,1,0:T(8,128)(2,1)}, f32[2,64,7,64]{3,2,1,0:T(8,128)S(1)}, f32[2,64,7,64]{3,2,1,0:T(8,128)S(1)}, f32[64,64,...) while((s32[]{:T(128)}, ...), condition=%wide.region_4.5_spmd, body=%wide.region_3.4_spmd.sunk | while | flops 8645296128 | bytes 159709520 | solution.py:99
  57.5 26.6 %fusion.476 = f32[64,7,64,256]{3,0,2,1:T(8,128)S(1)} fusion(f32[64,64,256,1]{2,1,0,3:T(8,128)S(1)} %bitcast.691, f32[64,7,64,1]{2,1,0,3:T(8,128)S(1)} %dynamic-slice_bitcast_fusion.16), kind=kOutput, calls=%fused_computation.6.clone.1 | convolution fusion | flops 5637144576 | bytes 33669120 | tf_op jit(solution)/shard_map/while/body/eval_jaxpr/ris,stk->ritk/dot_general | solution.py:88
  84.0 31.0 %fusion.477 = f32[64,7,7,256]{3,1,2,0:T(8,128)} fusion(f32[64,7,64,256]{3,0,2,1:T(8,128)S(1)} %fusion.476, f32[2,64,7,64]{3,2,1,0:T(8,128)S(1)} %get-tuple-element.1165, s32[]{:T(128)S(6)} %copy.391), kind=kOutput, calls=%fused_computation.clone.1 | convolution fusion | flops 616562688 | bytes 32833540 | tf_op jit(solution)/shard_map/while/body/eval_jaxpr/ritk,rjt->rijk/dot_general | solution.py:94
  187.7 26.5 %fusion.476 = f32[64,7,64,256]{3,0,2,1:T(8,128)S(1)} fusion(f32[64,64,256,1]{2,1,0,3:T(8,128)S(1)} %bitcast.691, f32[64,7,64,1]{2,1,0,3:T(8,128)S(1)} %dynamic-slice_bitcast_fusion.16), kind=kOutput, calls=%fused_computation.6.clone.1 | convolution fusion | flops 5637144576 | bytes 33669120 | tf_op jit(solution)/shard_map/while/body/eval_jaxpr/ris,stk->ritk/dot_general | solution.py:88
  214.2 31.0 %fusion.477 = f32[64,7,7,256]{3,1,2,0:T(8,128)} fusion(f32[64,7,64,256]{3,0,2,1:T(8,128)S(1)} %fusion.476, f32[2,64,7,64]{3,2,1,0:T(8,128)S(1)} %get-tuple-element.1165, s32[]{:T(128)S(6)} %copy.391), kind=kOutput, calls=%fused_computation.clone.1 | convolution fusion | flops 616562688 | bytes 32833540 | tf_op jit(solution)/shard_map/while/body/eval_jaxpr/ritk,rjt->rijk/dot_general | solution.py:94
  314.9 138.7 %all-gather.5.cloned.1.call-done = bf16[1,12544,1024]{2,1,0:T(8,128)(2,1)} async-done(((bf16[1,12544,256]{2,1,0:T(8,128)(2,1)}), bf16[1,12544,1024]{2,1,0:T(8,128)(2,1)}) %all-gather.5.cloned.1.call-update) | async-done | bytes 25690128 | tf_op jit(solution)/shard_map/all_gather | solution.py:226
  479.8 268.5 %while.55 = (s32[]{:T(128)}, bf16[2,64,7,7,256]{4,3,2,1,0:T(8,128)(2,1)}, f32[2,64,7,64]{3,2,1,0:T(8,128)S(1)}, f32[2,64,7,64]{3,2,1,0:T(8,128)S(1)}, f32[64,64,...) while((s32[]{:T(128)}, ...), condition=%wide.region_7.8_spmd, body=%wide.region_6.7_spmd.sunk | while | flops 8645296128 | bytes 159709520 | solution.py:99
  527.4 31.3 %fusion.500 = f32[64,7,7,256]{3,1,2,0:T(8,128)} fusion(f32[64,7,64,256]{3,0,2,1:T(8,128)S(1)} %fusion.499, f32[2,64,7,64]{3,2,1,0:T(8,128)S(1)} %get-tuple-element.1210, s32[]{:T(128)S(6)} %copy.397), kind=kOutput, calls=%fused_computation.37.clone.1 | convolution fusion | flops 616562688 | bytes 32833540 | tf_op jit(solution)/shard_map/while/body/eval_jaxpr/ritk,rjt->rijk/dot_general | solution.py:94
  657.7 31.3 %fusion.500 = f32[64,7,7,256]{3,1,2,0:T(8,128)} fusion(f32[64,7,64,256]{3,0,2,1:T(8,128)S(1)} %fusion.499, f32[2,64,7,64]{3,2,1,0:T(8,128)S(1)} %get-tuple-element.1210, s32[]{:T(128)S(6)} %copy.397), kind=kOutput, calls=%fused_computation.37.clone.1 | convolution fusion | flops 616562688 | bytes 32833540 | tf_op jit(solution)/shard_map/while/body/eval_jaxpr/ritk,rjt->rijk/dot_general | solution.py:94
  756.4 130.7 %all-gather.7.cloned.1.call-done = bf16[1,12544,1024]{2,1,0:T(8,128)(2,1)} async-done(((bf16[1,12544,256]{2,1,0:T(8,128)(2,1)}), bf16[1,12544,1024]{2,1,0:T(8,128)(2,1)}) %all-gather.7.cloned.1.call-update) | async-done | bytes 25690128 | tf_op jit(solution)/shard_map/all_gather | solution.py:226
  1012.2 263.6 %while.56 = (s32[]{:T(128)}, f32[64,64,256]{2,0,1:T(8,128)}, f32[32,32,256]{2,0,1:T(8,128)}, f32[16,16,256]{2,0,1:T(8,128)}, f32[8,8,256]{2,0,1:T(8,128)S(1)}, /...) while((s32[]{:T(128)}, f32[64,64,256]{2,0,1:T(8,128)}, ...), condition=%wide.region_14.15_spmd.clone, body=%wide.region_13.14_spmd.clone.sunk | while | flops 8645672960 | bytes 168419664 | solution.py:129
  1012.4 28.3 %fusion.520 = f32[64,64,7,256]{3,1,2,0:T(8,128)} fusion(f32[2,64,7,7,256]{4,3,2,1,0:T(8,128)} %get-tuple-element.1262, s32[]{:T(128)S(6)} %copy.406, f32[2,64,7,64]{3,2,1,0:T(8,128)} %get-tuple-element.1261), kind=kOutput, calls=%fused_computation.92.clone.1 | convolution fusion | flops 616562688 | bytes 33293312 | tf_op jit(solution)/shard_map/while/body/eval_jaxpr/rijk,rjt->ritk/dot_general | solution.py:118
  1040.7 43.9 %bitcast_add_fusion.10 = f32[64,64,256]{2,0,1:T(8,128)} fusion(f32[64,64,256]{2,0,1:T(8,128)} %get-tuple-element.1240, f32[64,64,7,256]{3,1,2,0:T(8,128)} %fusion.520, pred[]{:T(512)S(6)} %compare.6, f32[2,64,7,64]{1,3,2,0:T(8,128)} %get-tuple-element.1260, s32[]{:T(128)S(6)} %copy.406), kind=kOutput, calls=%fused_computation.83.clone.1 | convolution fusion | flops 5639241728 | bytes 37978116 | tf_op jit(solution)/shard_map/while/body/eval_jaxpr/ris,ritk->stk/dot_general | solution.py:123
  1142.7 28.1 %fusion.520 = f32[64,64,7,256]{3,1,2,0:T(8,128)} fusion(f32[2,64,7,7,256]{4,3,2,1,0:T(8,128)} %get-tuple-element.1262, s32[]{:T(128)S(6)} %copy.406, f32[2,64,7,64]{3,2,1,0:T(8,128)} %get-tuple-element.1261), kind=kOutput, calls=%fused_computation.92.clone.1 | convolution fusion | flops 616562688 | bytes 33293312 | tf_op jit(solution)/shard_map/while/body/eval_jaxpr/rijk,rjt->ritk/dot_general | solution.py:118
  1170.9 44.2 %bitcast_add_fusion.10 = f32[64,64,256]{2,0,1:T(8,128)} fusion(f32[64,64,256]{2,0,1:T(8,128)} %get-tuple-element.1240, f32[64,64,7,256]{3,1,2,0:T(8,128)} %fusion.520, pred[]{:T(512)S(6)} %compare.6, f32[2,64,7,64]{1,3,2,0:T(8,128)} %get-tuple-element.1260, s32[]{:T(128)S(6)} %copy.406), kind=kOutput, calls=%fused_computation.83.clone.1 | convolution fusion | flops 5639241728 | bytes 37978116 | tf_op jit(solution)/shard_map/while/body/eval_jaxpr/ris,ritk->stk/dot_general | solution.py:123
  1293.8 46.6 %reduce-scatter.5.cloned.1.call-done = bf16[12544,256]{1,0:T(8,128)(2,1)} async-done(((bf16[12544,1024]{1,0:T(8,128)(2,1)}), bf16[12544,256]{1,0:T(8,128)(2,1)}) %reduce-scatter.5.cloned.1.call-update) | async-done | bytes 6422544 | tf_op jit(solution)/shard_map/reduce_scatter | solution.py:299
  1340.5 426.9 %reduce-scatter.3.cloned.1.call-done = bf16[12544,256]{1,0:T(8,128)(2,1)} async-done(((bf16[12544,1024]{1,0:T(8,128)(2,1)}), bf16[12544,256]{1,0:T(8,128)(2,1)}) %reduce-scatter.3.cloned.1.call-update) | async-done | bytes 6422544 | tf_op jit(solution)/shard_map/reduce_scatter | solution.py:299
  1778.9 266.9 %while.57 = (s32[]{:T(128)}, f32[64,64,256]{2,0,1:T(8,128)}, f32[32,32,256]{2,0,1:T(8,128)}, f32[16,16,256]{2,0,1:T(8,128)S(1)}, f32[8,8,256]{2,0,1:T(8,128)}, /...) while((s32[]{:T(128)}, f32[64,64,256]{2,0,1:T(8,128)}, ...), condition=%wide.region_16.17_spmd.clone, body=%wide.region_15.16_spmd.clone.sunk | while | flops 8645672960 | bytes 169402864 | solution.py:129
  1779.4 28.1 %fusion.543 = f32[64,64,7,256]{3,1,2,0:T(8,128)} fusion(f32[2,64,7,7,256]{4,3,2,1,0:T(8,128)} %get-tuple-element.1310, s32[]{:T(128)S(6)} %copy.421, f32[2,64,7,64]{3,2,1,0:T(8,128)} %get-tuple-element.1309), kind=kOutput, calls=%fused_computation.145.clone.1 | convolution fusion | flops 616562688 | bytes 33293312 | tf_op jit(solution)/shard_map/while/body/eval_jaxpr/rijk,rjt->ritk/dot_general | solution.py:118
  1807.5 43.8 %bitcast_add_fusion.11 = f32[64,64,256]{2,0,1:T(8,128)} fusion(f32[64,64,256]{2,0,1:T(8,128)} %get-tuple-element.1288, f32[64,64,7,256]{3,1,2,0:T(8,128)} %fusion.543, pred[]{:T(512)S(6)} %compare.7, f32[2,64,7,64]{1,3,2,0:T(8,128)} %get-tuple-element.1308, s32[]{:T(128)S(6)} %copy.421), kind=kOutput, calls=%fused_computation.136.clone.1 | convolution fusion | flops 5639241728 | bytes 37978116 | tf_op jit(solution)/shard_map/while/body/eval_jaxpr/ris,ritk->stk/dot_general | solution.py:123
  1908.7 28.1 %fusion.543 = f32[64,64,7,256]{3,1,2,0:T(8,128)} fusion(f32[2,64,7,7,256]{4,3,2,1,0:T(8,128)} %get-tuple-element.1310, s32[]{:T(128)S(6)} %copy.421, f32[2,64,7,64]{3,2,1,0:T(8,128)} %get-tuple-element.1309), kind=kOutput, calls=%fused_computation.145.clone.1 | convolution fusion | flops 616562688 | bytes 33293312 | tf_op jit(solution)/shard_map/while/body/eval_jaxpr/rijk,rjt->ritk/dot_general | solution.py:118
  1936.9 44.1 %bitcast_add_fusion.11 = f32[64,64,256]{2,0,1:T(8,128)} fusion(f32[64,64,256]{2,0,1:T(8,128)} %get-tuple-element.1288, f32[64,64,7,256]{3,1,2,0:T(8,128)} %fusion.543, pred[]{:T(512)S(6)} %compare.7, f32[2,64,7,64]{1,3,2,0:T(8,128)} %get-tuple-element.1308, s32[]{:T(128)S(6)} %copy.421), kind=kOutput, calls=%fused_computation.136.clone.1 | convolution fusion | flops 5639241728 | bytes 37978116 | tf_op jit(solution)/shard_map/while/body/eval_jaxpr/ris,ritk->stk/dot_general | solution.py:123
  2064.2 43.8 %all-reduce = (f32[2,1024]{1,0:T(2,128)}, f32[2,1024]{1,0:T(2,128)}, f32[2,81]{1,0:T(2,128)}, f32[2,1024,4]{1,2,0:T(4,128)}, f32[2,4]{1,0:T(2,128)}) all-reduce(f32[2,1024]{1,0:T(2,128)S(1)} %pad_maximum_fusion.4, f32[2,1024]{1,0:T(2,128)S(1)} %pad_maximum_fusion.5, ...), channel_id=1, replica_groups=mesh['dp'=8,'mp'=4] {'dp','mp'}, use_global_device_ids=true, to_apply=%region_22.23 | all-reduce | flops 12458 | bytes 99664 | tf_op jit(solution)/shard_map/psum | solution.py:328
  2116.6 27.6 %all-reduce.5.cloned.1.call-done = bf16[2,12544,256]{2,1,0:T(8,128)(2,1)} async-done(((bf16[2,12544,256]{2,1,0:T(8,128)(2,1)}), bf16[2,12544,256]{2,1,0:T(8,128)(2,1)}) %all-reduce.5.cloned.1.call-update) | async-done | bytes 12845072 | tf_op jit(solution)/shard_map/psum | solution.py:327
  (631 shorter events, 841.9 us)
Async XLA Ops:
  7.2 446.4 %all-gather.5.cloned.1.call-start = ((), (), s32[]{:S(2)}) async-start(), calls=%async_computation.5 | async-start | bytes 32112640 | tf_op jit(solution)/shard_map/all_gather | solution.py:226
  17.6 869.5 %all-gather.7.cloned.1.call-start = ((), (), s32[]{:S(2)}) async-start(), calls=%async_computation.6 | async-start | bytes 32112640 | tf_op jit(solution)/shard_map/all_gather | solution.py:226
  18.3 1322.1 %reduce-scatter.5.cloned.1.call-start = ((), (), s32[]{:S(2)}) async-start(), calls=%async_computation.3 | async-start | bytes 32112640 | tf_op jit(solution)/shard_map/reduce_scatter | solution.py:299
  302.0 164.9 %copy-start.9 = (f32[2,64,7,64]{3,2,1,0:T(8,128)}, f32[2,64,7,64]{3,2,1,0:T(8,128)S(1)}, u32[]{:S(2)}) copy-start(f32[2,64,7,64]{3,2,1,0:T(8,128)S(1)} %get-tuple-element.1356) | copy-start | bytes 688132
  302.0 164.9 %copy-start.10 = (f32[2,64,7,32]{3,2,1,0:T(8,128)}, f32[2,64,7,32]{3,2,1,0:T(8,128)S(1)}, u32[]{:S(2)}) copy-start(f32[2,64,7,32]{3,2,1,0:T(8,128)S(1)} %get-tuple-element.1357) | copy-start | bytes 344068
  302.0 164.9 %copy-start.18 = (f32[2,64,7,64]{3,2,1,0:T(8,128)}, f32[2,64,7,64]{3,2,1,0:T(8,128)S(1)}, u32[]{:S(2)}) copy-start(f32[2,64,7,64]{3,2,1,0:T(8,128)S(1)} %get-tuple-element.1361) | copy-start | bytes 688132
  302.0 164.9 %copy-start.27 = (f32[2,64,7,16]{1,3,2,0:T(8,128)}, f32[2,64,7,16]{1,3,2,0:T(8,128)S(1)}, u32[]{:S(2)}) copy-start(f32[2,64,7,16]{1,3,2,0:T(8,128)S(1)} %get-tuple-element.1370) | copy-start | bytes 172036
  302.0 164.9 %copy-start.31 = (f32[2,64,7,16]{1,3,2,0:T(8,128)}, f32[2,64,7,16]{1,3,2,0:T(8,128)S(1)}, u32[]{:S(2)}) copy-start(f32[2,64,7,16]{1,3,2,0:T(8,128)S(1)} %get-tuple-element.1372) | copy-start | bytes 172036
  750.7 146.9 %copy-start.29 = (f32[2,64,7,16]{1,3,2,0:T(8,128)}, f32[2,64,7,16]{1,3,2,0:T(8,128)S(1)}, u32[]{:S(2)}) copy-start(f32[2,64,7,16]{1,3,2,0:T(8,128)S(1)} %get-tuple-element.1371) | copy-start | bytes 172036
  750.7 146.9 %copy-start.33 = (f32[2,64,7,16]{1,3,2,0:T(8,128)}, f32[2,64,7,16]{1,3,2,0:T(8,128)S(1)}, u32[]{:S(2)}) copy-start(f32[2,64,7,16]{1,3,2,0:T(8,128)S(1)} %get-tuple-element.1373) | copy-start | bytes 172036
  750.7 136.4 %copy-start.90 = (f32[1,1024]{1,0:T(1,128)S(1)}, f32[1,1024]{1,0:T(1,128)}, u32[]{:S(2)}) copy-start(f32[1,1024]{1,0:T(1,128)} %get-tuple-element.699) | copy-start | bytes 12292
  919.4 848.0 %reduce-scatter.3.cloned.1.call-start = ((), (), s32[]{:S(2)}) async-start(), calls=%async_computation.2 | async-start | bytes 32112640 | tf_op jit(solution)/shard_map/reduce_scatter | solution.py:299
  939.8 1174.2 %all-reduce.7.cloned.1.call-start = ((), (), s32[]{:S(2)}) async-start(), calls=%async_computation.7 | async-start | bytes 18219008 | tf_op jit(solution)/shard_map/psum | solution.py:328
  1012.4 72.3 %slice-start = ((s8[7340032]{0:T(1024)(128)(4,1)}), s8[3145728]{0:T(1024)(128)(4,1)S(1)}, s32[]{:S(2)}) async-start(s8[7340032]{0:T(1024)(128)(4,1)} %bitcast.687), calls=%async_computation.8 | async-start | bytes 6291456 | tf_op jit(solution)/shard_map/while
  1040.7 44.0 %slice-start.1 = ((s8[7340032]{0:T(1024)(128)(4,1)}), s8[4194304]{0:T(1024)(128)(4,1)S(1)}, s32[]{:S(2)}) async-start(s8[7340032]{0:T(1024)(128)(4,1)} %bitcast.687), calls=%async_computation.9 | async-start | bytes 8388608 | tf_op jit(solution)/shard_map/while
  1040.7 44.0 %copy-start.11 = (f32[2,64,7,32]{3,2,1,0:T(8,128)S(1)}, f32[2,64,7,32]{3,2,1,0:T(8,128)}, u32[]{:S(2)}) copy-start(f32[2,64,7,32]{3,2,1,0:T(8,128)} %get-tuple-element.1264) | copy-start | bytes 344068 | tf_op jit(solution)/shard_map/while
  1142.7 72.4 %slice-start = ((s8[7340032]{0:T(1024)(128)(4,1)}), s8[3145728]{0:T(1024)(128)(4,1)S(1)}, s32[]{:S(2)}) async-start(s8[7340032]{0:T(1024)(128)(4,1)} %bitcast.687), calls=%async_computation.8 | async-start | bytes 6291456 | tf_op jit(solution)/shard_map/while
  1170.9 44.2 %slice-start.1 = ((s8[7340032]{0:T(1024)(128)(4,1)}), s8[4194304]{0:T(1024)(128)(4,1)S(1)}, s32[]{:S(2)}) async-start(s8[7340032]{0:T(1024)(128)(4,1)} %bitcast.687), calls=%async_computation.9 | async-start | bytes 8388608 | tf_op jit(solution)/shard_map/while
  1170.9 44.2 %copy-start.11 = (f32[2,64,7,32]{3,2,1,0:T(8,128)S(1)}, f32[2,64,7,32]{3,2,1,0:T(8,128)}, u32[]{:S(2)}) copy-start(f32[2,64,7,32]{3,2,1,0:T(8,128)} %get-tuple-element.1264) | copy-start | bytes 344068 | tf_op jit(solution)/shard_map/while
  1275.8 868.4 %all-reduce.5.cloned.1.call-start = ((), (), s32[]{:S(2)}) async-start(), calls=%async_computation.4 | async-start | bytes 25690112 | tf_op jit(solution)/shard_map/psum | solution.py:327
  1779.4 71.9 %slice-start.2 = ((s8[7340032]{0:T(1024)(128)(4,1)}), s8[3145728]{0:T(1024)(128)(4,1)S(1)}, s32[]{:S(2)}) async-start(s8[7340032]{0:T(1024)(128)(4,1)} %bitcast.689), calls=%async_computation.10 | async-start | bytes 6291456 | tf_op jit(solution)/shard_map/while
  1908.7 72.3 %slice-start.2 = ((s8[7340032]{0:T(1024)(128)(4,1)}), s8[3145728]{0:T(1024)(128)(4,1)S(1)}, s32[]{:S(2)}) async-start(s8[7340032]{0:T(1024)(128)(4,1)} %bitcast.689), calls=%async_computation.10 | async-start | bytes 6291456 | tf_op jit(solution)/shard_map/while
  1936.9 44.1 %slice-start.3 = ((s8[7340032]{0:T(1024)(128)(4,1)}), s8[4194304]{0:T(1024)(128)(4,1)S(1)}, s32[]{:S(2)}) async-start(s8[7340032]{0:T(1024)(128)(4,1)} %bitcast.689), calls=%async_computation.11 | async-start | bytes 8388608 | tf_op jit(solution)/shard_map/while
  1936.9 44.2 %copy-start.14 = (f32[2,64,7,32]{3,2,1,0:T(8,128)S(1)}, f32[2,64,7,32]{3,2,1,0:T(8,128)}, u32[]{:S(2)}) copy-start(f32[2,64,7,32]{3,2,1,0:T(8,128)} %get-tuple-element.1312) | copy-start | bytes 344068 | tf_op jit(solution)/shard_map/while
  (170 other events, 1381.0 us)
Sparse Core Ops, SparseCore 0:
  17.7 435.8 all-gather.4
  455.7 431.3 all-gather.6
  919.5 420.9 reduce-scatter.4
  1342.7 424.5 reduce-scatter.2
  1773.7 190.0 all-reduce.6
  1967.7 176.4 all-reduce.4
where the time goes:
time: 2180 us; the launch traced here: 2170 us
  matrix products  1130 us (52%)
  waiting for transfers between devices  771 us (35%)
  local copies, waits for them, and re-layouts  106 us (5%)
  other arithmetic  70 us (3%)
  blocking collectives  43.8 us (2%)
  loops' own time  34.6 us (2%)
    reduce_scatter x2, waiting for transfers between devices, backward_section(): lax.psum_scatter(whole_grad.astype(jnp.bfloat16), 'mp', scatter_dimension...  474 us
    dot_general x16, matrix products, pool_one_block(): jnp.einsum('ritk,rjt->rijk', middle, cols_part[level_no], precision=lax.P...  302 us
    dot_general x16, matrix products, spread_one_block(): jnp.einsum('ris,ritk->stk', rows_part[level_no], middle, precision=lax.Pr...  288 us
    all_gather x2, waiting for transfers between devices, forward_section(): lax.all_gather(first_weight[section_no], 'mp', axis=1, tiled=True)  269 us
    dot_general x16, matrix products, spread_one_block(): jnp.einsum('rijk,rjt->ritk', grad_part, cols_part[level_no], precision=la...  223 us
    dot_general x16, matrix products, pool_one_block(): jnp.einsum('ris,stk->ritk', rows_part[level_no], maps_all[level_no], prec...  204 us
    dot_general x8, matrix products, fold_columns(): jnp.einsum('rh,fh->rf', cols_part, shard_piece[:, block_no * slice_width:...  47.8 us
    psum x1, blocking collectives, per_device(): lax.psum((stacked[1], stacked[2], stacked[3], stacked[4], stacked[5], sta...  43.8 us
  transfers between devices with their start and end apart: 6, of which 5 were waited for; matrix products, arithmetic and copies ran while one was open for 57% of the time, Pallas kernels for 0%

commit v1 on v0

v1 whole, which is shorter than its diff:
```python
import functools
import math

import jax
import jax.numpy as jnp
from jax import lax
from jax.experimental import pallas as pl
from jax.experimental.pallas import tpu as pltpu
from jax.sharding import Mesh
from jax.sharding import PartitionSpec as P

CH = 256
CLS = 81
POOL = 7
BINS = POOL * POOL
CANVAS = 256
FEAT = BINS * CH
LANE = 128
UNITS = FEAT // LANE
SIDES = [CANVAS // (4 << level_no) for level_no in range(4)]
CELLS = 5440
ROWS_IN = [16, 32, 16, 8]
OFFSET = [0, 4096, 5120, 5376]
COUNT = [4, 1, 1, 1]
GROUP = 16
SMALL = pl.CostEstimate(flops=1000, bytes_accessed=1000, transcendentals=0)


def hat(distance):
    return jnp.maximum(1.0 - jnp.abs(distance), 0.0)


def cell_block(level_no, block_no):
    cells = ROWS_IN[level_no] * SIDES[level_no]
    return pl.ds(pl.multiple_of(OFFSET[level_no] + block_no * cells, min(cells, CH)), cells)


def lane_points(params):
    width = BINS * GROUP
    flat = params[...].T[:8]
    pieces = []
    for unused in range(3):
        pieces.append(flat.astype(jnp.bfloat16))
        flat = flat - pieces[-1].astype(jnp.float32)
    region = lax.broadcasted_iota(jnp.int32, (GROUP, width), 0)
    lane = lax.broadcasted_iota(jnp.int32, (GROUP, width), 1)
    chosen = (region == (lane & (GROUP - 1))).astype(jnp.bfloat16)
    wide = sum(jnp.dot(piece, chosen, preferred_element_type=jnp.float32) for piece in pieces)
    bin_no = lax.broadcasted_iota(jnp.int32, (1, width), 1) // GROUP
    across = bin_no // POOL
    down = bin_no - across * POOL

    def place(begin, extent, number):
        fraction = (number.astype(jnp.float32) + 0.5) * (1.0 / POOL)
        return jnp.clip(begin + fraction * extent, 0.0, wide[4:5])

    return place(wide[0:1], wide[1:2], down), place(wide[2:3], wide[3:4], across), wide[5:6]


def spread_kernel(unit_places, scale, groups, bounds, params, first, second, out, table, stack):
    group_no = pl.program_id(0)
    col_row, row_row, level_row = lane_points(params)

    @pl.when(group_no == 0)
    def _():
        out[...] = jnp.zeros_like(out)

    def fill(grads):
        for unit_no in range(UNITS):
            bin_no, half = divmod(unit_no, 2)
            owner, place = unit_places[unit_no]
            stack[bin_no * GROUP : (bin_no + 1) * GROUP, half * LANE : (half + 1) * LANE] = grads[
                owner, :, place * LANE : (place + 1) * LANE
            ]

    @pl.when(group_no < groups)
    def _():
        fill(first)

    @pl.when(group_no >= groups)
    def _():
        fill(second)

    for level_no in range(4):
        side = SIDES[level_no]
        begin = bounds[group_no, level_no]
        finish = bounds[group_no, 4 + level_no]

        @pl.when(finish > begin)
        def _():
            span = lax.broadcasted_iota(jnp.int32, (side, BINS * GROUP), 0).astype(jnp.float32)
            table[:side] = jnp.where(level_row == level_no, hat(span - col_row) * scale, 0.0)

        many = ROWS_IN[level_no]

        def step(chunk_no, carry):
            first_row = chunk_no * many
            weights = jnp.concatenate(
                [
                    table[:side] * hat((first_row + row_no).astype(jnp.float32) - row_row)
                    for row_no in range(many)
                ],
                axis=0,
            ).astype(jnp.bfloat16)
            at = cell_block(level_no, chunk_no)
            out[at, :] += jnp.dot(weights, stack[...], preferred_element_type=jnp.float32)
            return carry

        lax.fori_loop(begin, finish, step, 0)


def gelu_slope(preact):
    scale = math.sqrt(2.0 / math.pi)
    square = preact * preact
    bent = jnp.tanh(scale * preact * (1.0 + 0.044715 * square))
    return 0.5 * (1.0 + bent) + 0.5 * preact * (1.0 - bent * bent) * scale * (
        1.0 + 3.0 * 0.044715 * square
    )


def region_params(corners, level):
    regions = level.shape[0]
    inverse = jnp.where(
        level < 0.5, 0.25, jnp.where(level < 1.5, 0.125, jnp.where(level < 2.5, 0.0625, 0.03125))
    )
    most = CANVAS * inverse - 1.0
    begin_col = corners[0] * inverse - 0.5
    begin_row = corners[1] * inverse - 0.5
    extent_col = (corners[2] - corners[0]) * inverse
    extent_row = (corners[3] - corners[1]) * inverse
    lane = lax.broadcasted_iota(jnp.int32, (regions, LANE), 1)
    params = jnp.zeros((regions, LANE), jnp.float32)
    for place, column in enumerate((begin_col, extent_col, begin_row, extent_row, most, level)):
        params = jnp.where(lane == place, column, params)

    one = begin_row + extent_row * (0.5 / POOL)
    other = begin_row + extent_row * ((POOL - 0.5) / POOL)
    low = jnp.floor(jnp.clip(jnp.minimum(one, other) - 0.001, 0.0, most))
    high = jnp.minimum(jnp.floor(jnp.clip(jnp.maximum(one, other) + 0.001, 0.0, most)) + 1.0, most)
    lane_level = (lane & 3).astype(jnp.float32)
    per_row = jnp.where(lane_level == 1.0, 1.0 / 32, jnp.where(lane_level == 3.0, 1.0 / 8, 1.0 / 16))
    member = level == lane_level
    low = jnp.where(member, jnp.floor(low * per_row), 64.0)
    high = jnp.where(member, jnp.floor(high * per_row) + 1.0, 0.0)
    groups = regions // GROUP
    low = jnp.min(low.reshape(groups, GROUP, LANE), axis=1)
    high = jnp.max(high.reshape(groups, GROUP, LANE), axis=1)
    lane = lax.broadcasted_iota(jnp.int32, (groups, LANE), 1)
    level_no = lane & 3
    limit = jnp.where(level_no == 0, float(COUNT[0]), 1.0)
    bounds = jnp.where(lane < 4, jnp.clip(low, 0.0, limit), jnp.clip(high, 0.0, limit))
    return params, bounds.astype(jnp.int32)


def columns_of(info, first, number=1):
    return [info[:, at : at + 1] for at in range(first, first + number)]


def head_kernel(
    factor, parts, first_bias, second_weight, second_bias, out_weight, out_bias, info,
    first_pre, second_pre, acts, heads, moved, params, bounds,
):
    hidden = first_bias.shape[1]
    pre = first_bias[...] + parts[0].astype(jnp.float32)
    for owner in range(1, parts.shape[0]):
        pre = pre + parts[owner].astype(jnp.float32)
    first_pre[...] = pre
    act = jax.nn.gelu(pre).astype(jnp.bfloat16)
    share = hidden // acts.shape[0]
    for owner in range(acts.shape[0]):
        acts[owner, :, :share] = act[:, owner * share : (owner + 1) * share]
    pre = jnp.dot(act, second_weight[...], preferred_element_type=jnp.float32) + second_bias[...]
    second_pre[...] = pre
    act = jax.nn.gelu(pre).astype(jnp.bfloat16)
    for owner in range(acts.shape[0]):
        acts[owner, :, share:] = act[:, owner * share : (owner + 1) * share]
    head = jnp.dot(act, out_weight[...], preferred_element_type=jnp.float32) + out_bias[...]
    heads[...] = head
    corners = columns_of(info, 0, 4)
    deltas = [head[:, CLS + at : CLS + at + 1] for at in range(4)]
    centre_col, centre_row, box_width, box_height = box_frame(corners)
    moved_col = centre_col + deltas[0] / (10.0 * factor) * box_width
    moved_row = centre_row + deltas[1] / (10.0 * factor) * box_height
    moved_width = box_width * jnp.exp(deltas[2] / (5.0 * factor))
    moved_height = box_height * jnp.exp(deltas[3] / (5.0 * factor))
    corners = (
        moved_col - 0.5 * moved_width,
        moved_row - 0.5 * moved_height,
        moved_col + 0.5 * moved_width,
        moved_row + 0.5 * moved_height,
    )
    table = info[...]
    lane = lax.broadcasted_iota(jnp.int32, table.shape, 1)
    for place, column in enumerate(corners):
        table = jnp.where(lane == place, column, table)
    moved[...] = table
    values, chunks = region_params(corners, info[:, 8:9])
    params[...] = values
    bounds[...] = chunks


def head_back_kernel(
    factor, first_pre, second_pre, heads, info, second_weight, out_weight, grads, probs
):
    hidden = first_pre.shape[1]
    corners = columns_of(info, 0, 4)
    truth = columns_of(info, 4, 4)
    label, live, live_count, moving = columns_of(info, 9, 4)
    centre_col, centre_row, box_width, box_height = box_frame(corners)
    truth_col, truth_row, truth_width, truth_height = box_frame(truth)
    goals = (
        10.0 * factor * (truth_col - centre_col) / box_width,
        10.0 * factor * (truth_row - centre_row) / box_height,
        5.0 * factor * jnp.log(truth_width / box_width),
        5.0 * factor * jnp.log(truth_height / box_height),
    )
    head = heads[...]
    lane = lax.broadcasted_iota(jnp.int32, head.shape, 1)
    logits = jnp.where(lane < CLS, head, -jnp.inf)
    shifted = jnp.exp(logits - jnp.max(logits, axis=1, keepdims=True))
    share = shifted / jnp.sum(shifted, axis=1, keepdims=True)
    probs[...] = share
    onehot = (lane == label.astype(jnp.int32)).astype(jnp.float32)
    goal = jnp.zeros_like(head)
    for place, column in enumerate(goals):
        goal = jnp.where(lane == CLS + place, column, goal)
    dhead = jnp.where(
        lane < CLS,
        live * (share - onehot) / live_count,
        jnp.where(
            lane < CLS + 4, moving * jnp.clip(head - goal, -1.0, 1.0) / live_count, 0.0
        ),
    ).astype(jnp.bfloat16)
    grads[:, 2 * hidden :] = dhead
    across = (((1,), (1,)), ((), ()))
    dact = lax.dot_general(dhead, out_weight[...], across, preferred_element_type=jnp.float32)
    dpre = (gelu_slope(second_pre[...]) * dact).astype(jnp.bfloat16)
    grads[:, hidden : 2 * hidden] = dpre
    dact = lax.dot_general(dpre, second_weight[...], across, preferred_element_type=jnp.float32)
    dact = dact.astype(jnp.bfloat16).astype(jnp.float32)
    grads[:, :hidden] = (gelu_slope(first_pre[...]) * dact).astype(jnp.bfloat16)


def plane_place(device, shard):
    return {"plane": lax.div(device, 2), "core": lax.rem(device, 2), "mp": shard}


def half_of(ref, which):
    size = ref.shape[0] // 2
    return ref.at[pl.ds(which * size, size)]


def plane_gather(chips, shard, source, target, sems, local_sem):
    core = lax.axis_index("core")
    chip = lax.axis_index("plane")
    me = chip * 2 + core

    def send(kind, block, place, target_chip, target_core):
        return pltpu.make_async_remote_copy(
            src_ref=block, dst_ref=place,
            send_sem=sems.at[0, kind], recv_sem=sems.at[1, kind],
            device_id=plane_place(target_chip * 2 + target_core, shard),
            device_id_type=pl.DeviceIdType.MESH,
        )

    def beside(kind, held):
        slot = held * 2 + core
        block = source if kind == 0 else target.at[slot]
        return send(kind, block, target.at[slot], chip, 1 - core)

    own = pltpu.make_async_copy(source, target.at[me], local_sem)

    if chips == 4:
        near = chip + 1 - 2 * lax.rem(chip, 2)
        other = lax.rem(chip + 2, 4)
        far = 3 - chip
        first = send(4, source, target.at[me], near, core)
        second = send(5, source, target.at[me], other, core)
        place = half_of(target.at[near * 2 + core], 0)
        first_on = send(6, place, place, other, core)
        place = half_of(target.at[other * 2 + core], 1)
        second_on = send(7, place, place, near, core)
        asides = [beside(kind, held) for kind, held in enumerate((chip, near, other, far))]

        def start():
            first.start()
            second.start()
            asides[0].start()
            own.start()

        def relay():
            first.wait_recv()
            first_on.start()
            second.wait_recv()
            second_on.start()
            asides[1].start()
            asides[2].start()

        def last():
            first_on.wait_recv()
            second_on.wait_recv()
            asides[3].start()

        def end():
            own.wait()
            for copy in (first, second, first_on, second_on):
                copy.wait_send()
            for copy in asides:
                copy.wait()

        return start, relay, last, end

    straight = [
        send(chips + step, source, target.at[me], lax.rem(chip + step, chips), core)
        for step in range(1, chips)
    ]
    asides = [beside(step, lax.rem(chip - step + chips, chips)) for step in range(chips)]

    def start():
        for copy in straight:
            copy.start()
        asides[0].start()
        own.start()

    def relay():
        for step in range(1, chips):
            straight[step - 1].wait_recv()
            asides[step].start()

    def last():
        pass

    def end():
        own.wait()
        for copy in straight:
            copy.wait_send()
        for copy in asides:
            copy.wait()

    return start, relay, last, end


def pool_one(group_no, unit_places, params, maps, out, cols, rows, table, total):
    place = pl.ds(pl.multiple_of(group_no * GROUP, GROUP), GROUP)
    begin_col, extent_col, begin_row, extent_row, most, level = [
        jnp.broadcast_to(params[place, at : at + 1], (GROUP, LANE)) for at in range(6)
    ]
    for bin_no in range(POOL):
        fraction = (bin_no + 0.5) / POOL
        cols[bin_no] = jnp.clip(begin_col + fraction * extent_col, 0.0, most)
        rows[bin_no] = jnp.clip(begin_row + fraction * extent_row, 0.0, most)
    lane = lax.broadcasted_iota(jnp.int32, (GROUP, LANE), 1)
    total[...] = jnp.zeros_like(total)
    for level_no in range(4):
        side = SIDES[level_no]
        span = (lane % side).astype(jnp.float32)
        for bin_no in range(POOL):
            table[bin_no] = jnp.where(level == level_no, hat(span - cols[bin_no]), 0.0)
        cells = ROWS_IN[level_no] * side

        def step(block_no, carry):
            first_row = (block_no * ROWS_IN[level_no]).astype(jnp.float32)
            tiles = []
            for tile in range(-(-cells // LANE)):
                at = (lane // side + tile * (LANE // side)).astype(jnp.float32) + first_row
                parts = []
                for i in range(POOL):
                    weight = hat(at - rows[i])
                    parts += [weight * table[j] for j in range(POOL)]
                tiles.append(jnp.concatenate(parts, axis=0).astype(jnp.bfloat16))
            weights = tiles[0] if len(tiles) == 1 else jnp.concatenate(tiles, axis=1)
            total[...] += jnp.dot(
                weights[:, :cells],
                maps[cell_block(level_no, block_no), :],
                preferred_element_type=jnp.float32,
            )
            return carry

        lax.fori_loop(0, COUNT[level_no], step, 0)
    for unit_no in range(UNITS):
        bin_no, half = divmod(unit_no, 2)
        owner, at = unit_places[unit_no]
        out[owner, place, at * LANE : (at + 1) * LANE] = total[
            bin_no * GROUP : (bin_no + 1) * GROUP, half * LANE : (half + 1) * LANE
        ].astype(jnp.bfloat16)


def weight_line(me, shard, first_weight, weight, line_sem, own_sem):
    shards, depth, width = weight.shape
    first_row = pl.multiple_of(jnp.minimum(me * depth, FEAT - depth), LANE)
    slice_here = first_weight.at[pl.ds(first_row, depth)]
    own = pltpu.make_async_copy(slice_here, weight.at[shard], own_sem)

    def send(way, step):
        if way == 0:
            block, target = lax.rem(shard - step + shards, shards), lax.rem(shard + 1, shards)
        else:
            block, target = lax.rem(shard + step, shards), lax.rem(shard + shards - 1, shards)
        return pltpu.make_async_remote_copy(
            src_ref=slice_here if step == 0 else weight.at[block], dst_ref=weight.at[block],
            send_sem=line_sem.at[0, way, step], recv_sem=line_sem.at[1, way, step],
            device_id=plane_place(me, target), device_id_type=pl.DeviceIdType.MESH,
        )

    def start():
        @pl.when(shard < shards - 1)
        def _():
            send(0, 0).start()

        @pl.when(shard > 0)
        def _():
            send(1, 0).start()

        own.start()

    def turn(step):
        @pl.when(shard >= step)
        def _():
            send(0, step - 1).wait_recv()

            @pl.when(shard < shards - 1)
            def _():
                send(0, step).start()

        @pl.when(shard + step < shards)
        def _():
            send(1, step - 1).wait_recv()

            @pl.when(shard > 0)
            def _():
                send(1, step).start()

    def end():
        own.wait()
        for step in range(shards):

            @pl.when(jnp.logical_and(shard >= step, shard < shards - 1))
            def _():
                send(0, step).wait_send()

            @pl.when(jnp.logical_and(shard + step < shards, shard > 0))
            def _():
                send(1, step).wait_send()

    return start, turn, end


def cascade_kernel(
    owners, shards,
    info, maps, first_weight, first_bias, second_weight, second_bias, out_weight, out_bias,
    moved, probs, all_params, all_bounds,
    first_back, second_back, slices, second_final, first_heads, second_heads,
    weights, second_held, pooled, gots, between, spare_probs, spare_params, spare_bounds,
    whole, sent, beside, added, parts, first_pre, second_pre, heads, grads, acts,
    grads_all, acts_all, own_sums, rising, falling, final, extra, mixed,
    cols, rows_at, table, total,
    line_sem, pooled_sem, side_sem, part_sem, grad_sem, acts_sem, back_sem, rise_sem, fall_sem,
    free_sem, slice_sem, mixed_sem, head_sem, local_sem,
):
    mesh_type = pl.DeviceIdType.MESH
    shard = lax.axis_index("mp")
    core = lax.axis_index("core")
    chip = lax.axis_index("plane")
    chips = owners // 2
    me = chip * 2 + core
    regions, hidden = first_pre.shape
    depth = pooled.shape[2]
    half = regions // 2
    rows, width = own_sums.shape[1:]
    each, unit_places = unit_table(owners)

    def peer(step):
        return lax.rem(me + step, owners)

    def chip_before(step):
        return lax.rem(chip - step + chips, chips)

    second_load = [
        pltpu.make_async_copy(second_weight.at[section], second_held, local_sem.at[0])
        for section in range(2)
    ]
    second_load[0].start()
    barrier = pltpu.get_barrier_semaphore()
    for step in range(1, owners):
        pl.semaphore_signal(
            barrier, inc=1, device_id=plane_place(peer(step), shard), device_id_type=mesh_type
        )
    for step in range(1, shards):
        pl.semaphore_signal(
            barrier, inc=1, device_id=plane_place(me, lax.rem(shard + step, shards)),
            device_id_type=mesh_type,
        )
    pl.semaphore_wait(barrier, owners + shards - 2)
    lines = [
        weight_line(
            me, shard, first_weight.at[section], weights.at[section], line_sem.at[section],
            local_sem.at[1 + section],
        )
        for section in range(2)
    ]

    def pooled_copy(section, step, side, batch):
        target = lax.rem(chip + step, chips) * 2 + (core if side == 0 else 1 - core)
        place = pl.ds(batch * half, half)
        at = 2 * step + side
        return pltpu.make_async_remote_copy(
            src_ref=pooled.at[target, place], dst_ref=gots.at[section, me, place],
            send_sem=pooled_sem.at[0, section, batch, at],
            recv_sem=pooled_sem.at[1, section, batch, at],
            device_id=plane_place(target, shard), device_id_type=mesh_type,
        )

    def pooled_own(section, batch):
        place = pl.ds(batch * half, half)
        return pltpu.make_async_copy(
            pooled.at[me, place], gots.at[section, me, place], local_sem.at[3 + batch]
        )

    def pooled_send(section, batch):
        for step in range(chips):
            for side in range(2):
                if step + side:
                    pooled_copy(section, step, side, batch).start()
        pooled_own(section, batch).start()

    def side_copy(section, step):
        source = chip_before(step)
        return pltpu.make_async_remote_copy(
            src_ref=sent.at[source], dst_ref=beside.at[source],
            send_sem=side_sem.at[0, section, step], recv_sem=side_sem.at[1, section, step],
            device_id=plane_place(chip * 2 + 1 - core, shard), device_id_type=mesh_type,
        )

    def part_copy(section, step):
        source = chip_before(step)
        return pltpu.make_async_remote_copy(
            src_ref=added.at[source], dst_ref=parts.at[chip],
            send_sem=part_sem.at[0, section, step], recv_sem=part_sem.at[1, section, step],
            device_id=plane_place(source * 2 + core, shard), device_id_type=mesh_type,
        )

    def acts_copy(section, step):
        target = peer(step)
        return pltpu.make_async_remote_copy(
            src_ref=acts.at[target], dst_ref=acts_all.at[me],
            send_sem=acts_sem.at[0, section, step], recv_sem=acts_sem.at[1, section, step],
            device_id=plane_place(target, shard), device_id_type=mesh_type,
        )

    def acts_own(section):
        return pltpu.make_async_copy(acts.at[me], acts_all.at[me], local_sem.at[5 + section])

    def multiply(section, source):
        place = pl.ds(source * 2, 2)
        block = gots[section, place].reshape(2 * regions, depth)

        def columns(at, carry):
            place = pl.ds(pl.multiple_of(at * width, LANE), width)
            product = jnp.dot(block, weights[section, at], preferred_element_type=jnp.float32)
            for which in range(2):
                part = product[which * regions : (which + 1) * regions]

                @pl.when(core == which)
                def _():
                    whole[source, :, place] = part

                @pl.when(core != which)
                def _():
                    sent[source, :, place] = part.astype(jnp.bfloat16)

            return carry

        lax.fori_loop(0, shards, columns, 0)

    def combine(section, step):
        source = chip_before(step)
        side_copy(section, step).wait_recv()
        added[source] = (whole[source] + beside[source].astype(jnp.float32)).astype(jnp.bfloat16)

        @pl.when(step > 0)
        def _():
            part_copy(section, step).start()

    def first_layer(section):
        for batch in range(2):
            pooled_own(section, batch).wait()

        def arrive(step, carry):
            for batch in range(2):

                @pl.when(step > 0)
                def _():
                    pooled_copy(section, step, 0, batch).wait_recv()

                pooled_copy(section, step, 1, batch).wait_recv()
            multiply(section, chip_before(step))
            side_copy(section, step).start()

            @pl.when(step > 0)
            def _():
                combine(section, step - 1)

            return carry

        lax.fori_loop(0, chips, arrive, 0)
        combine(section, chips - 1)

    def first_sums(section):
        def settle(step, carry):
            side_copy(section, step).wait_send()
            for batch in range(2):
                pooled_copy(section, step, 1, batch).wait_send()

                @pl.when(step > 0)
                def _():
                    pooled_copy(section, step, 0, batch).wait_send()

            @pl.when(step > 0)
            def _():
                part_copy(section, step).wait()

            return carry

        lax.fori_loop(0, chips, settle, 0)
        parts[chip] = added[chip]

    def gather_of(section):
        return plane_gather(
            chips, shard, grads, grads_all, grad_sem.at[section], local_sem.at[7 + section]
        )

    def head(section, table_in, table_out, params_out, bounds_out, probs_out):
        one = pl.ds(section, 1)
        head_kernel(
            section + 1.0, parts, first_bias.at[one], second_held, second_bias.at[one],
            out_weight.at[section], out_bias.at[one], table_in,
            first_pre, second_pre, acts, heads, table_out, params_out, bounds_out,
        )
        for step in range(1, owners):
            acts_copy(section, step).start()
        acts_own(section).start()
        head_back_kernel(
            section + 1.0, first_pre, second_pre, heads, table_in, second_held,
            out_weight.at[section], grads, probs_out,
        )

    def acts_end(section):
        acts_own(section).wait()
        for step in range(1, owners):
            acts_copy(section, step).wait()

    def pool(section, first, last):
        def step(group_no, carry):
            pool_one(
                group_no, unit_places, all_params.at[section], maps, pooled,
                cols, rows_at, table, total,
            )
            return carry

        lax.fori_loop(first, last, step, 0)

    groups = regions // GROUP
    quarter = groups // 4

    lines[0][0]()
    values, chunks = region_params(columns_of(info, 0, 4), info[:, 8:9])
    all_params[0] = values
    all_bounds[0] = chunks
    for owner in range(owners):
        taken = [place for who, place in unit_places if who == owner]
        for place in range(each):
            if place not in taken:
                pooled[owner, :, place * LANE : (place + 1) * LANE] = jnp.zeros(
                    (regions, LANE), jnp.bfloat16
                )
    pool(0, 0, 2 * quarter)
    pooled_send(0, 0)
    pool(0, 2 * quarter, 3 * quarter)
    if shards > 1:
        lines[0][1](1)
    pool(0, 3 * quarter, groups)
    pooled_send(0, 1)
    for step in range(2, shards):
        lines[0][1](step)
        if step == shards - 2:
            lines[1][0]()
    if shards < 4:
        lines[1][0]()
    lines[0][2]()
    second_load[0].wait()
    first_layer(0)
    if shards > 1:
        lines[1][1](1)
    first_sums(0)
    head(0, info, between, all_params.at[1], all_bounds.at[1], spare_probs)
    second_load[1].start()
    start, relay, last, end = gather_of(0)
    start()

    pool(1, 0, quarter)
    if shards > 2:
        lines[1][1](2)
    relay()
    pool(1, quarter, 2 * quarter)
    pooled_send(1, 0)
    last()
    pool(1, 2 * quarter, 3 * quarter)
    for step in range(3, shards):
        lines[1][1](step)
    end()
    acts_end(0)
    pool(1, 3 * quarter, groups)
    pooled_send(1, 1)
    stores = (own_sums, rising, falling)
    weight_gradient, chain_start, chain_step, chain_end, chain_settle = shard_sums(
        me, shard, shards, gots.at[0], grads_all, acts_all, *stores, final.at[0], extra,
        rise_sem, fall_sem,
    )
    return_multiply, return_start, return_settle = pooled_return(
        me, shard, grads_all, weights.at[0], gots.at[0], first_back, back_sem.at[0], local_sem.at[9]
    )
    weight_gradient()
    chain_start()
    return_multiply()
    lines[1][2]()
    second_load[1].wait()
    first_layer(1)
    chain_step(0, True)
    chain_step(0, False)
    first_sums(1)
    return_start()
    for number in range(1, shards // 2):
        chain_step(number, True)
        chain_step(number, False)
    head(1, between, moved, spare_params, spare_bounds, probs)
    start, relay, last, end = gather_of(1)
    start()
    for number in range(shards // 2, shards):
        chain_step(number, True)
        chain_step(number, False)
    relay()
    chain_end()
    chain_settle()

    @pl.when(shard > 0)
    def _():
        pl.semaphore_signal(
            free_sem.at[0], inc=1,
            device_id=plane_place(me, lax.rem(shard + shards - 1, shards)),
            device_id_type=mesh_type,
        )

    @pl.when(shard < shards - 1)
    def _():
        pl.semaphore_signal(
            free_sem.at[1], inc=1, device_id=plane_place(me, lax.rem(shard + 1, shards)),
            device_id_type=mesh_type,
        )

    last()
    acts_end(1)
    end()

    slice_gather = plane_gather(
        chips, shard, final.at[0, pl.ds(0, depth)], slices, slice_sem, local_sem.at[10]
    )
    second_kept = pltpu.make_async_copy(
        final.at[1, pl.ds(0, depth)], second_final, local_sem.at[11]
    )
    head_gathers = [
        plane_gather(
            chips, shard, mixed.at[section], target, head_sem.at[section],
            local_sem.at[12 + section],
        )
        for section, target in enumerate((first_heads, second_heads))
    ]

    def mixed_copy(section, step):
        target = lax.rem(shard + step, shards)
        return pltpu.make_async_remote_copy(
            src_ref=final.at[section, pl.ds(depth, rows - depth)],
            dst_ref=mixed.at[section, :, pl.ds(pl.multiple_of(shard * width, LANE), width)],
            send_sem=mixed_sem.at[0, section, step], recv_sem=mixed_sem.at[1, section, step],
            device_id=plane_place(me, target), device_id_type=mesh_type,
        )

    def mix_start(section):
        for step in range(1, shards):
            mixed_copy(section, step).start()
        for at in range(shards):

            @pl.when(shard == at)
            def _():
                mixed[section, :, at * width : (at + 1) * width] = final[section, depth:, :]

    def mix_end(section):
        for step in range(1, shards):
            mixed_copy(section, step).wait()

    weight_gradient, chain_start, chain_step, chain_end, chain_settle = shard_sums(
        me, shard, shards, gots.at[1], grads_all, acts_all, *stores, final.at[1], extra,
        rise_sem, fall_sem,
    )
    back_multiply, back_start, back_settle = pooled_return(
        me, shard, grads_all, weights.at[1], pooled, second_back, back_sem.at[1], local_sem.at[14]
    )
    mix_start(0)
    slice_gather[0]()
    weight_gradient()

    @pl.when(shard < shards - 1)
    def _():
        pl.semaphore_wait(free_sem.at[0], 1)

    @pl.when(shard > 0)
    def _():
        pl.semaphore_wait(free_sem.at[1], 1)

    chain_start()
    back_multiply()
    mix_end(0)
    head_gathers[0][0]()
    chain_step(0, True)
    slice_gather[1]()
    head_gathers[0][1]()
    back_start()
    chain_step(0, False)
    for number in range(1, shards):
        chain_step(number, True)
        chain_step(number, False)
    slice_gather[2]()
    head_gathers[0][2]()
    chain_end()
    mix_start(1)
    second_kept.start()
    mix_end(1)
    head_gathers[1][0]()
    head_gathers[1][1]()
    head_gathers[1][2]()
    second_kept.wait()
    slice_gather[3]()
    head_gathers[0][3]()
    head_gathers[1][3]()
    return_settle()
    back_settle()
    chain_settle()


def run_cascade(
    owners, shards, info, maps, first_weight, first_bias, second_weight, second_bias, out_weight,
    out_bias,
):
    regions = info.shape[0]
    hidden = first_bias.shape[1]
    each, unused = unit_table(owners)
    depth = each * LANE
    rows, width, share = sum_sizes(owners, shards, depth, hidden)
    wide = 2 * hidden + LANE
    chips = owners // 2
    bf16 = jnp.bfloat16
    f32 = jnp.float32
    dma = pltpu.SemaphoreType.DMA
    vmem = pl.BlockSpec(memory_space=pltpu.VMEM)
    hbm = pl.BlockSpec(memory_space=pl.ANY)
    block = (owners, regions, depth)
    heads = (owners, rows - depth, hidden)
    shapes = [
        ((regions, LANE), f32),
        ((regions, LANE), f32),
        ((2, regions, LANE), f32),
        ((2, regions // GROUP, LANE), jnp.int32),
        (block, bf16),
        (block, bf16),
        ((owners, depth, width), bf16),
        ((depth, width), bf16),
        (heads, bf16),
        (heads, bf16),
    ]
    scratch = [
        pltpu.VMEM((2, shards, depth, width), bf16),
        pltpu.VMEM((hidden, hidden), bf16),
        pltpu.VMEM(block, bf16),
        pltpu.VMEM((2, *block), bf16),
        pltpu.VMEM((regions, LANE), f32),
        pltpu.VMEM((regions, LANE), f32),
        pltpu.VMEM((regions, LANE), f32),
        pltpu.VMEM((regions // GROUP, LANE), jnp.int32),
        pltpu.VMEM((chips, regions, hidden), f32),
        pltpu.VMEM((chips, regions, hidden), bf16),
        pltpu.VMEM((chips, regions, hidden), bf16),
        pltpu.VMEM((chips, regions, hidden), bf16),
        pltpu.VMEM((chips, regions, hidden), bf16),
        pltpu.VMEM((regions, hidden), f32),
        pltpu.VMEM((regions, hidden), f32),
        pltpu.VMEM((regions, LANE), f32),
        pltpu.VMEM((regions, wide), bf16),
        pltpu.VMEM((owners, regions, 2 * share), bf16),
        pltpu.VMEM((owners, regions, wide), bf16),
        pltpu.VMEM((owners, regions, 2 * share), bf16),
        pltpu.VMEM((shards, rows, width), bf16),
        pltpu.VMEM((shards, rows, width), bf16),
        pltpu.VMEM((shards, rows, width), bf16),
        pltpu.VMEM((2, rows, width), bf16),
        pltpu.VMEM((rows - depth - share, width), f32),
        pltpu.VMEM((2, rows - depth, hidden), bf16),
        pltpu.VMEM((POOL, GROUP, LANE), f32),
        pltpu.VMEM((POOL, GROUP, LANE), f32),
        pltpu.VMEM((POOL, GROUP, LANE), f32),
        pltpu.VMEM((BINS * GROUP, CH), f32),
        dma((2, 2, 2, shards)),
        dma((2, 2, 2, owners)),
        dma((2, 2, chips)),
        dma((2, 2, chips)),
        dma((2, 2, owners)),
        dma((2, 2, owners)),
        dma((2, 2, owners)),
        dma((2, shards)),
        dma((2, shards)),
        pltpu.SemaphoreType.REGULAR((2,)),
        dma((2, owners)),
        dma((2, 2, shards)),
        dma((2, 2, owners)),
        dma((15,)),
    ]
    return pl.pallas_call(
        functools.partial(cascade_kernel, owners, shards),
        out_shape=[jax.ShapeDtypeStruct(*shape) for shape in shapes],
        in_specs=[vmem, vmem, hbm, vmem, hbm, vmem, vmem, vmem],
        out_specs=[vmem] * 4 + [hbm] * 6,
        scratch_shapes=scratch,
        compiler_params=pltpu.CompilerParams(
            vmem_limit_bytes=62 << 20, collective_id=1, has_side_effects=True
        ),
        cost_estimate=SMALL,
        name="cascade",
    )(info, maps, first_weight, first_bias, second_weight, second_bias, out_weight, out_bias)


def box_frame(corners):
    box_width = corners[2] - corners[0]
    box_height = corners[3] - corners[1]
    return (corners[0] + 0.5 * box_width, corners[1] + 0.5 * box_height, box_width, box_height)


def unit_table(owners):
    each = -(-UNITS // owners)
    firsts = [min(owner * each, UNITS - each) for owner in range(owners)]
    return each, [(unit_no // each, unit_no - firsts[unit_no // each]) for unit_no in range(UNITS)]


def spread_regions(bounds, params, first, second):
    bounds = bounds.reshape(-1, LANE)
    params = params.reshape(-1, LANE)
    groups = bounds.shape[0] // 2
    owners = first.shape[0]
    each, places = unit_table(owners)
    width = BINS * GROUP
    block = (owners, GROUP, each * LANE)
    return pl.pallas_call(
        functools.partial(spread_kernel, places, 1.0 / 3.0, groups),
        grid_spec=pltpu.PrefetchScalarGridSpec(
            num_scalar_prefetch=1,
            grid=(2 * groups,),
            in_specs=[
                pl.BlockSpec((GROUP, LANE), lambda g, b: (g, 0)),
                pl.BlockSpec(block, lambda g, b: (0, jnp.minimum(g, groups - 1), 0)),
                pl.BlockSpec(block, lambda g, b: (0, jnp.maximum(g - groups, 0), 0)),
            ],
            out_specs=pl.BlockSpec((CELLS, CH), lambda g, b: (0, 0)),
            scratch_shapes=[
                pltpu.VMEM((SIDES[0], width), jnp.float32),
                pltpu.VMEM((width, CH), jnp.bfloat16),
            ],
        ),
        out_shape=jax.ShapeDtypeStruct((CELLS, CH), jnp.float32),
        compiler_params=pltpu.CompilerParams(vmem_limit_bytes=48 << 20),
        cost_estimate=SMALL,
        name="spread_regions",
    )(bounds, params, first, second)


def row_step(rows):
    blocks = rows // 16
    return 16 * max(number for number in range(1, 21) if blocks % number == 0)


def shard_sums(
    me, shard, shards, pooled, grads, acts, own, rising, falling, final, extra, rise_sem, fall_sem
):
    owners, regions, depth = pooled.shape
    both = owners * regions
    width = own.shape[2]
    rows = own.shape[1]
    hidden = width * shards
    share = acts.shape[2] // 2
    mesh_type = pl.DeviceIdType.MESH

    def weight_gradient():
        over_rows = (((0,), (0,)), ((), ()))

        def lay(first, size, block):
            for at in range(shards):
                own[at, pl.ds(first, size), :] = block[
                    :, at * width : (at + 1) * width
                ].astype(jnp.bfloat16)

        early = jnp.maximum(me * depth - (FEAT - depth), 0)

        def features(first, size):
            block = lax.dot_general(
                pooled[:, :, pl.ds(first, size)].reshape(both, size),
                grads[:, :, :hidden].reshape(both, hidden),
                over_rows, preferred_element_type=jnp.float32,
            )
            lay(pl.multiple_of(lax.rem(first + 2 * depth - early, depth), LANE), size, block)

        def step(number, carry):
            features(pl.multiple_of(number * CH, CH), CH)
            return carry

        lax.fori_loop(0, depth // CH, step, 0)
        if depth % CH:
            features(depth - depth % CH, depth % CH)
        block = lax.dot_general(
            acts[:, :, :share].reshape(both, share),
            grads[:, :, hidden : 2 * hidden].reshape(both, hidden),
            over_rows, preferred_element_type=jnp.float32,
        )
        lay(depth, share, block)
        block = lax.dot_general(
            acts[:, :, share:].reshape(both, share),
            grads[:, :, 2 * hidden :].reshape(both, LANE),
            over_rows, preferred_element_type=jnp.float32,
        )
        sums = jnp.dot(
            jnp.ones((8, both), jnp.bfloat16), grads[...].reshape(both, 2 * hidden + LANE),
            preferred_element_type=jnp.float32,
        )
        part = share // shards
        for at in range(shards):
            extra[...] = jnp.zeros_like(extra)
            extra[:part, :LANE] = block[at * part : (at + 1) * part]
            for number in range((2 * hidden + LANE) // LANE):
                row, lane = (part + number, 0) if width == LANE else (number, LANE)
                extra[row : row + 1, lane : lane + LANE] = sums[
                    :1, number * LANE : (number + 1) * LANE
                ]
            own[at, depth + share :, :] = extra[...].astype(jnp.bfloat16)

    step_rows = row_step(rows)

    def by_rows(work):
        def step(number, carry):
            work(pl.ds(pl.multiple_of(number * step_rows, 16), step_rows))
            return carry

        lax.fori_loop(0, rows // step_rows, step, 0)

    def rise_copy(at):
        return pltpu.make_async_remote_copy(
            src_ref=rising.at[at], dst_ref=rising.at[at],
            send_sem=rise_sem.at[0, at], recv_sem=rise_sem.at[1, at],
            device_id=plane_place(me, lax.rem(shard + 1, shards)), device_id_type=mesh_type,
        )

    def fall_copy(at):
        return pltpu.make_async_remote_copy(
            src_ref=falling.at[at], dst_ref=falling.at[at],
            send_sem=fall_sem.at[0, at], recv_sem=fall_sem.at[1, at],
            device_id=plane_place(me, lax.rem(shard + shards - 1, shards)),
            device_id_type=mesh_type,
        )

    def add_own(at, stream):
        def work(place):
            stream[at, place, :] = (
                stream[at, place, :].astype(jnp.float32)
                + own[at, place, :].astype(jnp.float32)
            ).astype(jnp.bfloat16)

        by_rows(work)

    def rise_first(at):
        return pltpu.make_async_remote_copy(
            src_ref=own.at[at], dst_ref=rising.at[at],
            send_sem=rise_sem.at[0, at], recv_sem=rise_sem.at[1, at],
            device_id=plane_place(me, lax.rem(shard + 1, shards)), device_id_type=mesh_type,
        )

    def fall_first(at):
        return pltpu.make_async_remote_copy(
            src_ref=own.at[at], dst_ref=falling.at[at],
            send_sem=fall_sem.at[0, at], recv_sem=fall_sem.at[1, at],
            device_id=plane_place(me, lax.rem(shard + shards - 1, shards)),
            device_id_type=mesh_type,
        )

    def chain_start():
        for number in range(shards - 1):
            at = shards - 1 - number

            @pl.when(shard == 0)
            def _():
                rise_first(at).start()

            @pl.when(shard == shards - 1)
            def _():
                fall_first(number).start()

    def pass_on(at, stream, copy, ahead):
        @pl.when(ahead)
        def _():
            copy(at).wait_recv()
            add_own(at, stream)
            copy(at).start()

    def chain_step(number, near):
        up = shards - 1 - number
        down = number
        low = shard < shards // 2
        rises = low if near else jnp.logical_not(low)
        falls = jnp.logical_not(rises)
        inner = jnp.logical_and(shard > 0, shard < shards - 1)
        rises = jnp.logical_and(rises, jnp.logical_and(inner, shard < up))
        falls = jnp.logical_and(falls, jnp.logical_and(inner, shard > down))
        pass_on(up, rising, rise_copy, rises)
        pass_on(down, falling, fall_copy, falls)

    def chain_end():
        def work(place):
            final[place, :] = own[shard, place, :]

        def work_up(place):
            total = own[shard, place, :].astype(jnp.float32)
            total = total + rising[shard, place, :].astype(jnp.float32)
            final[place, :] = total.astype(jnp.bfloat16)

        def work_down(place):
            total = own[shard, place, :].astype(jnp.float32)
            total = total + falling[shard, place, :].astype(jnp.float32)
            final[place, :] = total.astype(jnp.bfloat16)

        def work_both(place):
            total = own[shard, place, :].astype(jnp.float32)
            total = total + rising[shard, place, :].astype(jnp.float32)
            total = total + falling[shard, place, :].astype(jnp.float32)
            final[place, :] = total.astype(jnp.bfloat16)

        if shards == 1:
            by_rows(work)
            return

        @pl.when(shard > 0)
        def _():
            rise_copy(shard).wait_recv()

        @pl.when(shard < shards - 1)
        def _():
            fall_copy(shard).wait_recv()

        @pl.when(shard == 0)
        def _():
            by_rows(work_down)

        @pl.when(shard == shards - 1)
        def _():
            by_rows(work_up)

        @pl.when(jnp.logical_and(shard > 0, shard < shards - 1))
        def _():
            by_rows(work_both)

    def chain_settle():
        for at in range(shards):

            @pl.when(jnp.logical_and(shard < at, shard == 0))
            def _():
                rise_first(at).wait_send()

            @pl.when(jnp.logical_and(shard < at, shard > 0))
            def _():
                rise_copy(at).wait_send()

            @pl.when(jnp.logical_and(shard > at, shard == shards - 1))
            def _():
                fall_first(at).wait_send()

            @pl.when(jnp.logical_and(shard > at, shard < shards - 1))
            def _():
                fall_copy(at).wait_send()

    return weight_gradient, chain_start, chain_step, chain_end, chain_settle


def pooled_return(me, shard, grads, weight, sent, back, back_sem, own_sem):
    owners, regions, depth = sent.shape
    shards, unused, width = weight.shape
    both = owners * regions

    def back_copy(step):
        target = lax.rem(me + step, owners)
        return pltpu.make_async_remote_copy(
            src_ref=sent.at[target], dst_ref=back.at[me],
            send_sem=back_sem.at[0, step], recv_sem=back_sem.at[1, step],
            device_id=plane_place(target, shard), device_id_type=pl.DeviceIdType.MESH,
        )

    own = pltpu.make_async_copy(sent.at[me], back.at[me], own_sem)

    def multiply():
        def columns(first, size):
            at = pl.ds(first, size)
            block = sum(
                lax.dot_general(
                    grads[:, :, part * width : (part + 1) * width].reshape(both, width),
                    weight[part, at, :],
                    (((1,), (1,)), ((), ())),
                    preferred_element_type=jnp.float32,
                )
                for part in range(shards)
            )
            sent[:, :, at] = block.astype(jnp.bfloat16).reshape(owners, regions, size)

        def step(number, carry):
            columns(pl.multiple_of(number * CH, CH), CH)
            return carry

        lax.fori_loop(0, depth // CH, step, 0)
        if depth % CH:
            columns(depth - depth % CH, depth % CH)

    def start():
        for step in range(1, owners):
            back_copy(step).start()
        own.start()

    def settle():
        own.wait()

        def work(step, carry):
            back_copy(step).wait()
            return carry

        lax.fori_loop(1, owners, work, 0)

    return multiply, start, settle


def sum_sizes(owners, shards, depth, hidden):
    width = hidden // shards
    share = hidden // owners
    part = share // shards
    extra = max(part, 32) if width > LANE else part + 32
    return depth + share + -(-extra // 16) * 16, width, share


def widen_kernel(every, *refs):
    refs[-1][0] = every[...].astype(jnp.float32)


def widen_slices(every, section_no, whole=None):
    owners, depth, width = every.shape
    rows = FEAT // 7
    given = () if whole is None else (whole,)
    return pl.pallas_call(
        widen_kernel,
        grid=(7,),
        in_specs=[pl.BlockSpec((rows, width), lambda at: (at, 0))]
        + [pl.BlockSpec(memory_space=pl.ANY)] * len(given),
        out_specs=pl.BlockSpec((1, rows, width), lambda at: (section_no, at, 0)),
        out_shape=jax.ShapeDtypeStruct((2, FEAT, width), jnp.float32),
        input_output_aliases={1: 0} if given else {},
        cost_estimate=SMALL,
        name="widen_slices",
    )(every.reshape(owners * depth, width), *given)


def widen_heads_kernel(share, shards, first, second, second_grad, out_grad, sums):
    owners = first.shape[0]
    part = share // shards
    width = first.shape[2] // shards
    for section, heads in enumerate((first, second)):
        for owner in range(owners):
            rows = slice(owner * share, (owner + 1) * share)
            second_grad[section, rows, :] = heads[owner, :share].astype(jnp.float32)
            for at in range(shards):
                rows = slice(owner * share + at * part, owner * share + (at + 1) * part)
                out_grad[section, rows, :] = heads[
                    owner, share : share + part, at * width : at * width + LANE
                ].astype(jnp.float32)
        row, lane = (share, LANE) if width > LANE else (share + part, 0)
        sums[section] = heads[0, row : row + sums.shape[1], lane : lane + LANE].astype(jnp.float32)


def widen_heads(share, shards, first, second):
    hidden = first.shape[2]
    count = -(-(2 * hidden + LANE) // (LANE * 8)) * 8
    return pl.pallas_call(
        functools.partial(widen_heads_kernel, share, shards),
        out_shape=[
            jax.ShapeDtypeStruct((2, hidden, hidden), jnp.float32),
            jax.ShapeDtypeStruct((2, hidden, LANE), jnp.float32),
            jax.ShapeDtypeStruct((2, count, LANE), jnp.float32),
        ],
        compiler_params=pltpu.CompilerParams(vmem_limit_bytes=48 << 20),
        cost_estimate=SMALL,
        name="widen_heads",
    )(first, second)


def per_device(
    pyramid,
    proposals,
    levels,
    labels,
    targets,
    buckets,
    first_weight,
    first_bias,
    second_weight,
    second_bias,
    class_weight,
    class_bias,
    box_weight,
    box_bias,
):
    owners = lax.axis_size("plane") * 2
    shards = lax.axis_size("mp")
    regions = levels.shape[1]
    hidden = first_bias.shape[1]
    share = hidden // owners

    index = jnp.arange(regions, dtype=jnp.int32)
    live = (index < regions // 2 + buckets[0] * (regions // 8)).astype(jnp.int32)
    order = (levels[0] * 1024 + proposals[0, 1] + proposals[0, 3]) * regions + index
    rank = jnp.sum((order[:, None] > order[None, :]).astype(jnp.int32), axis=1)
    moved = rank[None, :] == index[:, None]
    live_count = jnp.broadcast_to(jnp.sum(live), live.shape)
    moving = live * (labels[0] > 0).astype(jnp.int32)
    columns = jnp.concatenate(
        [proposals[0], targets[0], levels, labels, live[None], live_count[None], moving[None]],
        axis=0,
    ).astype(jnp.float32)
    info = jnp.sum(jnp.where(moved[:, None, :], columns[None], 0.0), axis=2)
    info = jnp.pad(info, ((0, 0), (0, LANE - columns.shape[0])))

    out_width = ((0, 0), (0, 0), (0, LANE - CLS - 4))
    out_weight = jnp.pad(jnp.concatenate([class_weight, box_weight], axis=2), out_width)
    out_bias = jnp.pad(jnp.concatenate([class_bias, box_bias], axis=1), out_width[1:])

    decoded_info, probs, params, bounds, *rest = run_cascade(
        owners, shards, info, pyramid[0], first_weight, first_bias, second_weight, second_bias,
        out_weight, out_bias,
    )
    first_back, second_back, first_all, second_final, *heads = rest
    pyramid_part = spread_regions(bounds, params, first_back, second_back)
    second_all = lax.all_gather(second_final, ("plane", "core"), axis=0)
    weight_total = widen_slices(first_all, 0)
    weight_total = widen_slices(second_all, 1, weight_total)
    second_grad, out_grad, sums = widen_heads(share, shards, *heads)
    sums = sums.reshape(2, -1)
    result = jnp.concatenate([probs[:, :CLS], decoded_info[:, :4]], axis=1)
    result = jnp.einsum(
        "pr,pc->rc", moved.astype(jnp.float32), result, precision=lax.Precision.HIGHEST
    )
    return (
        result[None, :, :CLS],
        result[:, CLS:].T[None],
        pyramid_part[None],
        weight_total,
        sums[:, :hidden],
        second_grad,
        sums[:, hidden : 2 * hidden],
        out_grad[:, :, :CLS],
        sums[:, 2 * hidden : 2 * hidden + CLS],
        out_grad[:, :, CLS : CLS + 4],
        sums[:, 2 * hidden + CLS : 2 * hidden + CLS + 4],
    )


def solution(mesh):
    chips = mesh.shape["dp"] // 2
    layout = Mesh(
        mesh.devices.reshape(chips, 2, mesh.shape["mp"]), ("plane", "core", "mp")
    )
    images = ("plane", "core", "mp")
    rows = P(images, None, None)
    columns = P(None, None, "mp")
    return jax.shard_map(
        per_device,
        mesh=layout,
        in_specs=(rows, rows, P(images, None), P(images, None), rows, P(images), columns)
        + (P(),) * 7,
        out_specs=(rows, rows, rows, columns) + (P(),) * 7,
        check_vma=False,
    )
```

time: 2180 us -> 423 us (0.19)
  matrix products: 1130 us -> 0.32 us
  waiting for transfers between devices: 771 us -> 3.57 us
  Pallas kernels: 0 us -> 380 us
  local copies, waits for them, and re-layouts: 106 us -> 12.7 us
  other arithmetic: 70 us -> 5.81 us
  blocking collectives: 43.8 us -> 0 us
  loops' own time: 34.6 us -> 0 us
    dot_general x94 -> x1, matrix products: 1130 us -> 0.32 us  [per_device(): jnp.einsum('pr,pc->rc', moved.astype(jnp.float32), result, precision=lax....]
    reduce_scatter x2 -> x0, waiting for transfers between devices: 474 us -> none  [backward_section(): lax.psum_scatter(whole_grad.astype(jnp.bfloat16), 'mp', scatter_dimension...]
    pallas_call x0 -> x5, Pallas kernels: none -> 380 us  [the longest x1 330 us: run_cascade(): pl.pallas_call(functools.partial(cascade_kernel, owners, shards), out_sha...]
    all_gather x2 -> x1, waiting for transfers between devices: 269 us -> 3.56 us  [per_device(): second_all = lax.all_gather(second_final, ('plane', 'core'), axis=0)]
    psum x1 -> x0, blocking collectives: 43.8 us -> none  [per_device(): lax.psum((stacked[1], stacked[2], stacked[3], stacked[4], stacked[5], sta...]
    another operation x4 -> x0, loops' own time: 34.6 us -> none  [the longest x2 22.4 us: pool_rows(): lax.map(pool_one_block, (block_split(row_tables, block), block_split(col_...]
    psum x2 -> x0, waiting for transfers between devices: 27.6 us -> none  [the longest x1 27.6 us: per_device(): lax.psum(stacked[0].astype(jnp.bfloat16), 'dp').astype(jnp.float32)]
  transfers between devices with their start and end apart: 6 -> 1, of which waited for: 5 -> 1; matrix products, arithmetic and copies ran while one was open for 57% -> 1% of each run, Pallas kernels for 0% -> 10%
where the time goes in v1:
time: 423 us; the launch traced here: 417 us
  Pallas kernels  380 us (90%)
  between operations  14.8 us (3%)
  local copies, waits for them, and re-layouts  12.7 us (3%)
  other arithmetic  5.81 us (1%)
    pallas_call x1, Pallas kernels, run_cascade(): pl.pallas_call(functools.partial(cascade_kernel, owners, shards), out_sha...  330 us
    pallas_call x1, Pallas kernels, spread_regions(): pl.pallas_call(functools.partial(spread_kernel, places, 1.0 / 3.0, groups...  26.1 us
    pallas_call x2, Pallas kernels, widen_slices(): pl.pallas_call(widen_kernel, grid=(7,), in_specs=[pl.BlockSpec((rows, wid...  17.6 us
  transfers between devices with their start and end apart: 1, of which 1 were waited for; matrix products, arithmetic and copies ran while one was open for 1% of the time, Pallas kernels for 10%

profile of v1, /device:TPU:0, one launch (start us, length us, event | category | flops | bytes accessed | tf_op | source)
XLA Modules:
  0.0 417.4 jit_solution(11673251935329583584)
XLA Ops:
  7.9 0.6 fusion.7
  8.5 0.8 fusion.12
  9.3 0.8 fusion.11
  10.0 0.7 compare_select_fusion
  10.7 0.6 broadcast_in_dim_broadcast_in_dim.3
  11.4 1.4 concatenate.22
  13.4 1.0 copy.33
  14.4 1.4 copy.32
  15.8 0.6 pad.12.info
  16.4 1.1 fusion.2.out_weight
  17.6 1.3 select_maximum_fusion.out_bias
  18.9 330.4 %cascade.1 = (f32[128,128]{1,0:T(8,128)}, f32[128,128]{1,0:T(8,128)}, f32[2,128,128]{2,1,0:T(8,128)}, s32[2,8,128]{2,1,0:T(8,128)}, bf16[8,128,1664]{2,1,0:T(8,1...) custom-call(f32[128,128]{1,0:T(8,128)} %pad.12.info, ...), custom_call_target="tpu_custom_call" | custom-call | flops 1000 | bytes 1000 | tf_op jit(solution)/shard_map/cascade/pallas_call | solution.py:925
  349.4 8.8 %widen_slices.2.refs_0_ = f32[2,12544,256]{2,1,0:T(8,128)} custom-call(bf16[13312,256]{1,0:T(8,128)(2,1)} %bitcast.53), custom_call_target="tpu_custom_call" | custom-call | flops 1000 | bytes 1000 | tf_op jit(solution)/shard_map/widen_slices/pallas_call | solution.py:1265
  358.2 1.9 copy-done.1
  360.1 6.1 %widen_heads.1 = (f32[2,1024,1024]{2,1,0:T(8,128)}, f32[2,1024,128]{2,1,0:T(8,128)S(1)}, f32[2,24,128]{2,1,0:T(8,128)S(1)}) custom-call(bf16[8,160,1024]{2,1,0:T(8,128)(2,1)S(1)} %copy-done.1, bf16[8,160,1024]{2,1,0:T(8,128)(2,1)} %get-tuple-element.33.second), custom_call_target="tpu_custom_call" | custom-call | flops 1000 | bytes 1000 | tf_op jit(solution)/shard_map/widen_heads/pallas_call | solution.py:1298
  366.2 26.1 %spread_regions.1 = f32[5440,256]{1,0:T(8,128)} custom-call(s32[16,128]{1,0:T(8,128)S(1)} %bitcast.52, f32[256,128]{1,0:T(8,128)S(1)} %bitcast.50, bf16[8,128,1664]{2,1,0:T(8,128)(2,1)S(1)} %copy-done, bf16[8,128,1664]{2,1,0:T(8,128)(2,1)} %get-tuple-element.29.second), custom_call_target="tpu_custom_call" | custom-call | flops 1000 | bytes 1000 | tf_op jit(solution)/shard_map/spread_regions/pallas_call | solution.py:959
  392.9 0.6 slice.53
  393.9 0.7 copy.34
  394.9 1.2 copy.35
  396.1 0.9 copy.36
  397.0 0.6 slice_bitcast_fusion.1
  397.6 0.6 fusion.14
  398.2 3.6 all-gather.3.cloned.1.call-done.every
  401.8 8.8 %widen_slices.3 = f32[2,12544,256]{2,1,0:T(8,128)} custom-call(bf16[13312,256]{1,0:T(8,128)(2,1)} %all-gather.3.cloned.1.call-done.every, f32[2,12544,256]{2,1,0:T(8,128)} %widen_slices.2.refs_0_), custom_call_target="tpu_custom_call", output_to_operand_aliasing={{}: (1, {})} | custom-call | flops 1000 | bytes 1000 | tf_op jit(solution)/shard_map/widen_slices/pallas_call | solution.py:1265
  (24 shorter events, 1.9 us)
Async XLA Ops:
  7.2 394.6 %all-gather.3.cloned.1.call-start = ((), (), s32[]{:S(2)}) async-start(), calls=%async_computation | async-start | bytes 7667712 | tf_op jit(solution)/shard_map/all_gather | solution.py:1357
  349.4 16.8 %copy-start.2 = (f32[2,128,128]{2,1,0:T(8,128)S(1)}, f32[2,128,128]{2,1,0:T(8,128)}, u32[]{:S(2)}) copy-start(f32[2,128,128]{2,1,0:T(8,128)} %get-tuple-element.27) | copy-start | bytes 393220
  349.4 16.8 %copy-start.3 = (s32[2,8,128]{2,1,0:T(8,128)S(1)}, s32[2,8,128]{2,1,0:T(8,128)}, u32[]{:S(2)}) copy-start(s32[2,8,128]{2,1,0:T(8,128)} %get-tuple-element.26) | copy-start | bytes 24580
  358.2 8.0 %copy-start = (bf16[8,128,1664]{2,1,0:T(8,128)(2,1)S(1)}, bf16[8,128,1664]{2,1,0:T(8,128)(2,1)}, u32[]{:S(2)}) copy-start(bf16[8,128,1664]{2,1,0:T(8,128)(2,1)} %get-tuple-element.28.first) | copy-start | bytes 10223620
  358.2 1.9 copy-start.1
  366.2 27.3 %copy-start.4 = (f32[128,128]{1,0:T(8,128)S(1)}, f32[128,128]{1,0:T(8,128)}, u32[]{:S(2)}) copy-start(f32[128,128]{1,0:T(8,128)} %get-tuple-element.25) | copy-start | bytes 196612
  366.2 27.3 %copy-start.5 = (f32[128,128]{1,0:T(8,128)S(1)}, f32[128,128]{1,0:T(8,128)}, u32[]{:S(2)}) copy-start(f32[128,128]{1,0:T(8,128)} %get-tuple-element.24) | copy-start | bytes 196612
Sparse Core Ops, SparseCore 0:
  349.5 52.2 all-gather.2
